TPU v7x, 32 devices: a whole 2x2x4 slice. The times are simulated.
32 devices in a mesh: ctx: 8 (over z, x), dp: 4 (over y, core).
Axes of the slice: x: 2, y: 2, z: 4, core: 2. Of those that a mesh axis runs over, the one named last changes fastest.
Arguments:
- tokens: bfloat16 [4, 4096, 512], P('dp', 'ctx'), may hold values from -6 to 6
- segment_ids: int32 [4, 4096], P('dp', 'ctx'), may hold values from 0 to 3, never falling along the last dimension, each value on 1 to 2048 neighbouring positions
- w_query: bfloat16 [512, 512], replicated, may hold values from -0.25 to 0.25
- w_key: bfloat16 [512, 512], replicated, may hold values from -0.25 to 0.25
- w_value: bfloat16 [512, 512], replicated, may hold values from -0.25 to 0.25
- w_out: bfloat16 [512, 512], replicated, may hold values from -0.25 to 0.25
- grad_out: bfloat16 [4, 4096, 512], P('dp', 'ctx'), may hold values from -6 to 6
Outputs:
- input_grad: bfloat16 [4, 4096, 512], P('dp', 'ctx')
- grad_w_query: bfloat16 [512, 512], replicated
- grad_w_key: bfloat16 [512, 512], replicated
- grad_w_value: bfloat16 [512, 512], replicated
- grad_w_out: bfloat16 [512, 512], replicated
Inputs may be any that keep to these rules, and one draw needn't show every extreme that they name: `segment_ids`: each drive log is a run of consecutive tokens of at most 2048 tokens.
All inputs are finite; a program needn't handle non-finite values.
Results may differ from a plain program's by a relative error of at most 0.006.
The roundings to bfloat16 on the way count: a program that leaves them out, or rounds other values in their place, can miss the bound.
Values may be sent and summed in bfloat16 or wider, within the bound.
A program may use at most 64 MiB of HBM per device.

v0:
```python
import jax
import jax.numpy as jnp
from jax import lax
from jax.sharding import PartitionSpec as P

H = 8
HD = 64
WINDOW = 128


def extended(block, sides, width):
    for axis, dim in sides:
        count = lax.axis_size(axis)
        forward = [(i, i + 1) for i in range(count - 1)]
        backward = [(target, source) for source, target in forward]
        low = lax.ppermute(
            lax.slice_in_dim(block, block.shape[dim] - width, None, axis=dim), axis, forward
        )
        high = lax.ppermute(lax.slice_in_dim(block, 0, width, axis=dim), axis, backward)
        block = jnp.concatenate([low, block, high], axis=dim)
    return block


def shifted(block, axis, distance):
    devices = range(lax.axis_size(axis))
    route = [(i - distance, i) for i in devices if i - distance in devices]
    return lax.ppermute(block, axis, route)


def project(left, weight):
    return jnp.dot(left, weight, preferred_element_type=jnp.float32).astype(jnp.bfloat16)


def matmul(left, right):
    return jnp.dot(left, right, preferred_element_type=jnp.float32)


def split_heads(values, length):
    return jnp.transpose(values.reshape(length, H, HD), (1, 0, 2))


def join_heads(values, length):
    return jnp.transpose(values, (1, 0, 2)).reshape(length, H * HD)


def on_device(tokens, segment_ids, w_query, w_key, w_value, w_out, grad_out):
    rows = tokens[0]
    seg = segment_ids[0]
    dout = grad_out[0]
    span = rows.shape[0]
    width = rows.shape[1]
    window = WINDOW
    keys_len = span + 2 * window
    place = lax.axis_index("ctx")
    count = lax.axis_size("ctx")
    query = project(rows, w_query)
    keyed = project(rows, w_key)
    valued = project(rows, w_value)
    dattn = project(dout, w_out.T)
    joined, seg_all = (
        extended(jnp.concatenate([keyed, valued], 1), (("ctx", 0),), window),
        extended(seg, (("ctx", 0),), window),
    )
    keys_all = joined[:, :width]
    values_all = joined[:, width:]
    valid = jnp.concatenate(
        [
            jnp.full((window,), place > 0),
            jnp.ones((span,), bool),
            jnp.full((window,), place < count - 1),
        ]
    )
    query_pos = jnp.arange(span, dtype=jnp.int32)
    key_pos = jnp.arange(keys_len, dtype=jnp.int32) - window
    near = jnp.abs(query_pos[:, None] - key_pos[None, :]) <= window
    mask = (seg[:, None] == seg_all[None, :]) & valid[None, :] & near
    scale = float(HD) ** (-0.5)

    def head_step(inputs):
        head_query, head_dattn, head_keys, head_values = inputs
        score = matmul(head_query, head_keys.T) * scale
        score = jnp.where(mask, score, -1e30)
        top = jnp.max(score, axis=-1, keepdims=True)
        weight = jnp.where(mask, jnp.exp(score - top), 0.0)
        prob = weight / jnp.sum(weight, axis=-1, keepdims=True)
        probb = prob.astype(jnp.bfloat16)
        attended = matmul(probb, head_values).astype(jnp.bfloat16)
        dprob = matmul(head_dattn, head_values.T)
        delta = jnp.sum(head_dattn.astype(jnp.float32) * attended.astype(jnp.float32), axis=-1)
        dscore = (prob * (dprob - delta[:, None])).astype(jnp.bfloat16)
        dquery = (matmul(dscore, head_keys) * scale).astype(jnp.bfloat16)
        dkey = (matmul(dscore.T, head_query) * scale).astype(jnp.bfloat16)
        dvalue = matmul(probb.T, head_dattn).astype(jnp.bfloat16)
        return (attended, dquery, dkey, dvalue)

    attended, dquery, dkey, dvalue = lax.map(
        head_step,
        (
            split_heads(query, span),
            split_heads(dattn, span),
            split_heads(keys_all, keys_len),
            split_heads(values_all, keys_len),
        ),
    )
    attended = join_heads(attended, span)
    grad_wo = matmul(attended.T, dout)
    dquery = join_heads(dquery, span)
    dkey = join_heads(dkey, keys_len)
    dvalue = join_heads(dvalue, keys_len)
    key_lower, key_own, key_upper = (
        dkey[:window],
        dkey[window : window + span],
        dkey[window + span :],
    )
    value_lower, value_own, value_upper = (
        dvalue[:window],
        dvalue[window : window + span],
        dvalue[window + span :],
    )
    total = matmul(dquery, w_query.T) + matmul(key_own, w_key.T) + matmul(value_own, w_value.T)
    grad_wq = matmul(rows.T, dquery)
    grad_wk = matmul(rows.T, key_own)
    grad_wv = matmul(rows.T, value_own)
    first_rows = rows[:window]
    last_rows = rows[span - window :]
    from_upper = shifted(jnp.concatenate([key_lower, value_lower], 1), "ctx", -1)
    from_lower = shifted(jnp.concatenate([key_upper, value_upper], 1), "ctx", 1)
    upper_key = from_upper[:, :width]
    upper_value = from_upper[:, width:]
    lower_key = from_lower[:, :width]
    lower_value = from_lower[:, width:]
    at_end = matmul(upper_key, w_key.T) + matmul(upper_value, w_value.T)
    at_start = matmul(lower_key, w_key.T) + matmul(lower_value, w_value.T)
    total = (
        total
        + jnp.pad(at_end, ((span - window, 0), (0, 0)))
        + jnp.pad(at_start, ((0, span - window), (0, 0)))
    )
    grad_wk = grad_wk + matmul(last_rows.T, upper_key) + matmul(first_rows.T, lower_key)
    grad_wv = grad_wv + matmul(last_rows.T, upper_value) + matmul(first_rows.T, lower_value)
    sum_q, sum_k, sum_v, sum_o = lax.psum((grad_wq, grad_wk, grad_wv, grad_wo), ("ctx", "dp"))
    return (
        total.astype(jnp.bfloat16)[None],
        sum_q.astype(jnp.bfloat16),
        sum_k.astype(jnp.bfloat16),
        sum_v.astype(jnp.bfloat16),
        sum_o.astype(jnp.bfloat16),
    )


def solution(mesh):
    return jax.shard_map(
        on_device,
        mesh=mesh,
        in_specs=(P("dp", "ctx", None), P("dp", "ctx"), P(), P(), P(), P(), P("dp", "ctx", None)),
        out_specs=(P("dp", "ctx", None), P(), P(), P(), P()),
        check_vma=False,
    )
```

profile of v0, /device:TPU:0, one launch (start us, length us, event | category | flops | bytes accessed | tf_op | source)
XLA Modules:
  0.0 232.5 jit_solution(5156802190297821747)
XLA Ops:
  0.7 1.8 convolution_convert_fusion.3
  3.8 4.8 %collective-permute-start = (bf16[128,1024]{0,1:T(8,128)(2,1)}, bf16[128,1024]{0,1:T(8,128)(2,1)S(1)}, u32[]{:S(2)}, u32[]{:S(2)}) collective-permute-start(bf16[128,1024]{0,1:T(8,128)(2,1)} %get-tuple-element.137), channel_id=1, source_target_pairs={{0,4},{4,8},{8,12},{12,16},{16,20},{20,24},{24,28},{1,5},{5,9},{9,... | collective-permute-start | bytes 786440 | tf_op jit(solution)/shard_map/ppermute | solution.py:16
  8.7 1.3 collective-permute-start.1
  10.0 4.5 %collective-permute-start.2 = (s32[128]{0:T(128)S(1)}, s32[128]{0:T(128)S(1)}, u32[]{:S(2)}, u32[]{:S(2)}) collective-permute-start(s32[128]{0:T(128)S(1)} %get-tuple-element.143), channel_id=1, source_target_pairs={{0,4},{4,8},{8,12},{12,16},{16,20},{20,24},{24,28},{1,5},{5,9},{9,... | collective-permute-start | bytes 1544 | tf_op jit(solution)/shard_map/ppermute | solution.py:16
  14.5 1.3 collective-permute-start.3
  17.0 1.3 copy.12
  18.3 1.9 collective-permute-done.2
  20.4 1.1 pad_maximum_fusion
  22.5 1.6 copy.13
  24.1 1.8 copy.14
  25.9 80.5 %while.17 = (s32[]{:T(128)}, bf16[8,512,64]{1,2,0:T(8,128)(2,1)}, bf16[8,512,64]{1,2,0:T(8,128)(2,1)}, bf16[8,768,64]{1,2,0:T(8,128)(2,1)}, bf16[8,768,64]{1,2,0...) while((s32[]{:T(128)}, bf16[8,512,64]{1,2,0:T(8,128)(2,1)}, ...), condition=%wide.region_4.5_spmd.clone, body=%wide.region_0.4_spmd.clone.sunk | while | flops 314948096 | bytes 15120777 | solution.py:96
  25.9 1.9 fusion.116
  31.3 1.8 fusion.120
  33.1 1.9 fusion.119
  36.0 1.9 fusion.116
  41.3 1.9 fusion.120
  43.2 1.9 fusion.119
  46.0 1.9 fusion.116
  51.4 1.9 fusion.120
  53.3 1.9 fusion.119
  56.1 1.9 fusion.116
  61.5 1.8 fusion.120
  63.3 1.9 fusion.119
  66.2 1.9 fusion.116
  71.5 1.8 fusion.120
  73.4 1.9 fusion.119
  76.2 1.9 fusion.116
  81.6 1.8 fusion.120
  83.5 1.9 fusion.119
  86.3 1.9 fusion.116
  91.7 1.8 fusion.120
  93.5 1.9 fusion.119
  96.3 1.9 fusion.116
  101.7 1.9 fusion.120
  103.6 1.9 fusion.119
  106.4 1.1 fusion.72
  108.7 1.4 convolution_bitcast_fusion
  110.7 1.4 collective-permute-start.4
  112.2 5.5 %collective-permute-start.5 = (bf16[128,1024]{0,1:T(8,128)(2,1)S(1)}, bf16[128,1024]{0,1:T(8,128)(2,1)S(1)}, u32[]{:S(2)}, u32[]{:S(2)}) collective-permute-start(bf16[128,1024]{0,1:T(8,128)(2,1)S(1)} %pad_maximum_fusion.4), channel_id=1, source_target_pairs={{0,4},{4,8},{8,12},{12,16},{16,20},{20,24},{24,28},{1,5},{5,9},{9,... | collective-permute-start | bytes 786440 | tf_op jit(solution)/shard_map/ppermute | solution.py:27
  118.1 1.4 fusion.40
  120.8 6.3 %collective-permute-done.5 = bf16[128,1024]{0,1:T(8,128)(2,1)S(1)} collective-permute-done((bf16[128,1024]{0,1:T(8,128)(2,1)S(1)}, bf16[128,1024]{0,1:T(8,128)(2,1)S(1)}, u32[]{:S(2)}, u32[]{:S(2)}) %collective-permute-start.5) | collective-permute-done | bytes 262176 | tf_op jit(solution)/shard_map/ppermute | solution.py:27
  127.0 1.3 fusion.37
  128.6 1.3 fusion.38
  129.8 94.0 %all-reduce.4 = (bf16[512,512]{0,1:T(8,128)(2,1)}, bf16[512,512]{0,1:T(8,128)(2,1)}, bf16[512,512]{0,1:T(8,128)(2,1)}, bf16[512,512]{1,0:T(8,128)(2,1)}) all-reduce(f32[512,512]{0,1:T(8,128)} %convolution_bitcast_fusion, f32[512,512]{0,1:T(8,128)} %fusion.38, f32[512,512]{0,1:T(8,128)} %fusion.37, ...), channel_id=1, replica_groups=mesh['ctx'=8,'dp'=4] {'ctx','dp'}, use_global_device_ids=true, to_apply=%region_5.6 | all-reduce | flops 1048576 | bytes 6291456 | tf_op jit(solution)/shard_map/psum | solution.py:141
  223.8 2.1 copy.15
  225.9 2.0 copy.16
  227.9 2.0 copy.17
  231.2 1.3 fusion.39
  (107 shorter events, 43.2 us)
Async XLA Ops:
  0.6 1.8 copy-start
  0.6 1.8 copy-start.1
  2.5 7.5 %copy-start.11 = (s32[1,512]{1,0:T(1,128)S(1)}, s32[1,512]{1,0:T(1,128)}, u32[]{:S(2)}) copy-start(s32[1,512]{1,0:T(1,128)} %param.10) | copy-start | bytes 6148
  2.5 13.4 %copy-start.3 = (bf16[512,512]{1,0:T(8,128)(2,1)S(1)}, bf16[512,512]{1,0:T(8,128)(2,1)}, u32[]{:S(2)}) copy-start(bf16[512,512]{1,0:T(8,128)(2,1)} %param.11) | copy-start | bytes 1572868
  3.0 13.4 %copy-start.5 = (bf16[1,512,512]{2,1,0:T(8,128)(2,1)S(1)}, bf16[1,512,512]{2,1,0:T(8,128)(2,1)}, u32[]{:S(2)}) copy-start(bf16[1,512,512]{2,1,0:T(8,128)(2,1)} %param.15) | copy-start | bytes 1572868
  3.0 13.4 %copy-start.9 = (bf16[512,512]{1,0:T(8,128)(2,1)S(1)}, bf16[512,512]{1,0:T(8,128)(2,1)}, u32[]{:S(2)}) copy-start(bf16[512,512]{1,0:T(8,128)(2,1)} %param.14) | copy-start | bytes 1572868
  3.8 16.6 %collective-permute-start = (bf16[128,1024]{0,1:T(8,128)(2,1)}, bf16[128,1024]{0,1:T(8,128)(2,1)S(1)}, u32[]{:S(2)}, u32[]{:S(2)}) collective-permute-start(bf16[128,1024]{0,1:T(8,128)(2,1)} %get-tuple-element.137), channel_id=1, source_target_pairs={{0,4},{4,8},{8,12},{12,16},{16,20},{20,24},{24,28},{1,5},{5,9},{9,... | collective-permute-start | bytes 786440 | tf_op jit(solution)/shard_map/ppermute | solution.py:16
  8.7 11.8 %collective-permute-start.1 = (bf16[128,1024]{0,1:T(8,128)(2,1)}, bf16[128,1024]{0,1:T(8,128)(2,1)}, u32[]{:S(2)}, u32[]{:S(2)}) collective-permute-start(bf16[128,1024]{0,1:T(8,128)(2,1)} %get-tuple-element.138), channel_id=1, source_target_pairs={{4,0},{8,4},{12,8},{16,12},{20,16},{24,20},{28,24},{5,1},{9,5},{13... | collective-permute-start | bytes 786440 | tf_op jit(solution)/shard_map/ppermute | solution.py:19
  10.0 10.2 %collective-permute-start.2 = (s32[128]{0:T(128)S(1)}, s32[128]{0:T(128)S(1)}, u32[]{:S(2)}, u32[]{:S(2)}) collective-permute-start(s32[128]{0:T(128)S(1)} %get-tuple-element.143), channel_id=1, source_target_pairs={{0,4},{4,8},{8,12},{12,16},{16,20},{20,24},{24,28},{1,5},{5,9},{9,... | collective-permute-start | bytes 1544 | tf_op jit(solution)/shard_map/ppermute | solution.py:16
  14.5 5.9 %collective-permute-start.3 = (s32[128]{0:T(128)S(1)}, s32[128]{0:T(128)S(1)}, u32[]{:S(2)}, u32[]{:S(2)}) collective-permute-start(s32[128]{0:T(128)S(1)} %get-tuple-element.144), channel_id=1, source_target_pairs={{4,0},{8,4},{12,8},{16,12},{20,16},{24,20},{28,24},{5,1},{9,5},{13... | collective-permute-start | bytes 1544 | tf_op jit(solution)/shard_map/ppermute | solution.py:19
  106.4 2.2 copy-start.8
  106.4 2.3 %copy-start.7 = (bf16[8,512,64]{1,2,0:T(8,128)(2,1)S(1)}, bf16[8,512,64]{1,2,0:T(8,128)(2,1)}, u32[]{:S(2)}) copy-start(bf16[8,512,64]{1,2,0:T(8,128)(2,1)} %get-tuple-element.60) | copy-start | bytes 1572868
  108.7 1.5 copy-start.4
  110.7 7.4 %copy-start.6 = (bf16[1,512,512]{2,1,0:T(8,128)(2,1)S(1)}, bf16[1,512,512]{2,1,0:T(8,128)(2,1)}, u32[]{:S(2)}) copy-start(bf16[1,512,512]{2,1,0:T(8,128)(2,1)} %param.15) | copy-start | bytes 1572868
  110.7 7.4 %copy-start.10 = (bf16[8,512,64]{1,2,0:T(8,128)(2,1)S(1)}, bf16[8,512,64]{1,2,0:T(8,128)(2,1)}, u32[]{:S(2)}) copy-start(bf16[8,512,64]{1,2,0:T(8,128)(2,1)} %get-tuple-element.63) | copy-start | bytes 1572868
  110.7 9.8 %collective-permute-start.4 = (bf16[128,1024]{0,1:T(8,128)(2,1)S(1)}, bf16[128,1024]{0,1:T(8,128)(2,1)S(1)}, u32[]{:S(2)}, u32[]{:S(2)}) collective-permute-start(bf16[128,1024]{0,1:T(8,128)(2,1)S(1)} %pad_maximum_fusion.3), channel_id=1, source_target_pairs={{4,0},{8,4},{12,8},{16,12},{20,16},{24,20},{28,24},{5,1},{9,5},{13... | collective-permute-start | bytes 786440 | tf_op jit(solution)/shard_map/ppermute | solution.py:27
  112.2 14.9 %collective-permute-start.5 = (bf16[128,1024]{0,1:T(8,128)(2,1)S(1)}, bf16[128,1024]{0,1:T(8,128)(2,1)S(1)}, u32[]{:S(2)}, u32[]{:S(2)}) collective-permute-start(bf16[128,1024]{0,1:T(8,128)(2,1)S(1)} %pad_maximum_fusion.4), channel_id=1, source_target_pairs={{0,4},{4,8},{8,12},{12,16},{16,20},{20,24},{24,28},{1,5},{5,9},{9,... | collective-permute-start | bytes 786440 | tf_op jit(solution)/shard_map/ppermute | solution.py:27
  223.8 6.2 %copy-start.2 = (bf16[512,512]{1,0:T(8,128)(2,1)S(1)}, bf16[512,512]{1,0:T(8,128)(2,1)}, u32[]{:S(2)}) copy-start(bf16[512,512]{1,0:T(8,128)(2,1)} %param.13) | copy-start | bytes 1572868
where the time goes:
time: 234 us; the launch traced here: 233 us
  blocking collectives  94 us (40%)
  matrix products  77.8 us (33%)
  starting transfers between devices  18.9 us (8%)
  other arithmetic  18 us (8%)
  local copies, waits for them, and re-layouts  14.2 us (6%)
  waiting for transfers between devices  8.38 us (4%)
    psum x1, blocking collectives, on_device(): lax.psum((grad_wq, grad_wk, grad_wv, grad_wo), ('ctx', 'dp'))  94 us
    dot_general x63, matrix products, matmul(): return jnp.dot(left, right, preferred_element_type=jnp.float32)  74.6 us
    ppermute x2, starting transfers between devices, extended(): lax.ppermute(lax.slice_in_dim(block, block.shape[dim] - width, None, axis...  9.39 us
    reduce_sum x8, other arithmetic, head_step(): prob = weight / jnp.sum(weight, axis=-1, keepdims=True)  8.47 us
    div x8, other arithmetic, head_step(): prob = weight / jnp.sum(weight, axis=-1, keepdims=True)  7.25 us
    ppermute x2, starting transfers between devices, shifted(): return lax.ppermute(block, axis, route)  6.88 us
    unnamed x27, local copies, waits for them, and re-layouts  6.26 us
    ppermute x2, waiting for transfers between devices, shifted(): return lax.ppermute(block, axis, route)  6.26 us
  transfers between devices with their start and end apart: 6, of which 3 were waited for; matrix products, arithmetic and copies ran while one was open for 2% of the time, Pallas kernels for 0%

commit v1 on v0

v1 whole, which is shorter than its diff:
```python
import functools

import jax
import jax.numpy as jnp
from jax import lax
from jax.experimental import pallas as pl
from jax.experimental.pallas import tpu as pltpu
from jax.sharding import PartitionSpec as P

HD = 64
WINDOW = 128
PAIR = 128
TILE_ROWS = 16
MESH = pl.DeviceIdType.MESH
F32 = jnp.float32
BF16 = jnp.bfloat16


def nn(left, right):
    return lax.dot_general(left, right, (((1,), (0,)), ((), ())), preferred_element_type=F32)


def nt(left, right):
    return lax.dot_general(left, right, (((1,), (1,)), ((), ())), preferred_element_type=F32)


def tn(left, right):
    return lax.dot_general(left, right, (((0,), (0,)), ((), ())), preferred_element_type=F32)


def wrap(index, count):
    return lax.rem(index + count, count)


def kernel(
    n_ctx, n_dp, reduced,
    tok, seg_row, w_q, w_k, w_v, w_o, dout,
    out, grads,
    halo, seg_halo, seg_own, tok_t, query, dattn, keyed, valued, bias,
    dq, dk, dv, acc_k, acc_v, att,
    side_send, side_recv,
    total, send, recv_a, recv_b, recv_c, recv_d,
    halo_s, halo_r, seg_s, seg_r, side_s, side_r, rs_s, rs_r, ag_s, ag_r,
):
    span, width = tok.shape
    win = WINDOW
    blocks = span // win
    pairs = width // PAIR
    ctx = lax.axis_index("ctx")
    dp = lax.axis_index("dp")
    up = (wrap(ctx + 1, n_ctx), dp)
    down = (wrap(ctx - 1, n_ctx), dp)

    core = lax.rem(dp, 2)
    y = lax.div(dp, 2)
    x = lax.rem(ctx, 2)
    z = lax.div(ctx, 2)
    nz = n_ctx // 2
    to_core = (ctx, dp + 1 - 2 * core)
    to_y = (ctx, lax.rem(dp + 2, 4))
    to_x = (ctx + 1 - 2 * x, dp)

    def to_z(step):
        return (lax.rem(ctx + 2 * step, n_ctx), dp)

    partners = [up, down]
    if reduced:
        partners += [to_core, to_y] + [to_z(step) for step in range(1, nz)]
    barrier = pltpu.get_barrier_semaphore()
    for partner in partners:
        pl.semaphore_signal(barrier, inc=1, device_id=partner, device_id_type=MESH)

    seg_own[...] = jnp.broadcast_to(seg_row[...], seg_own.shape)
    pl.semaphore_wait(barrier, len(partners))

    def remote(src, dst, s, r, device):
        copy = pltpu.make_async_remote_copy(
            src_ref=src, dst_ref=dst, send_sem=s, recv_sem=r, device_id=device, device_id_type=MESH
        )
        copy.start()
        return copy

    first = [
        remote(tok.at[pl.ds(span - win, win)], halo.at[0], halo_s.at[0], halo_r.at[0], up),
        remote(tok.at[pl.ds(0, win)], halo.at[1], halo_s.at[1], halo_r.at[1], down),
        remote(seg_own, seg_halo.at[0], seg_s.at[0], seg_r.at[0], up),
        remote(seg_own, seg_halo.at[1], seg_s.at[1], seg_r.at[1], down),
    ]

    query[...] = nn(tok[...], w_q[...]).astype(BF16)
    keyed[pl.ds(win, span)] = nn(tok[...], w_k[...]).astype(BF16)
    valued[pl.ds(win, span)] = nn(tok[...], w_v[...]).astype(BF16)
    dattn[...] = nt(dout[...], w_o[...]).astype(BF16)
    tok_t[:, pl.ds(win, span)] = tok[...].T

    for copy in first:
        copy.wait()
    for side, start in ((0, 0), (1, win + span)):
        rows = halo[side]
        keyed[pl.ds(start, win)] = nn(rows, w_k[...]).astype(BF16)
        valued[pl.ds(start, win)] = nn(rows, w_v[...]).astype(BF16)
        tok_t[:, pl.ds(start, win)] = rows.T

    own = seg_row[...].astype(F32)
    low = jnp.where(ctx > 0, seg_halo[0, 0:1, span - win :].astype(F32), -1.0)
    high = jnp.where(ctx < n_ctx - 1, seg_halo[1, 0:1, :win].astype(F32), -1.0)
    seg_all = jnp.concatenate([low, own, high], axis=1)
    q_pos = lax.broadcasted_iota(jnp.int32, (win, 3 * win), 0)
    k_pos = lax.broadcasted_iota(jnp.int32, (win, 3 * win), 1)
    near = (k_pos >= q_pos) & (k_pos <= q_pos + 2 * win)
    for i in range(blocks):
        column = jnp.broadcast_to(own[:, i * win : (i + 1) * win], (win, win)).T
        column = jnp.concatenate([column] * 3, axis=1)
        same = column == seg_all[:, i * win : (i + 3) * win]
        bias[i] = jnp.where(near & same, 0.0, -1e30)

    scale = float(HD) ** (-0.5)
    lane = lax.broadcasted_iota(jnp.int32, (win, PAIR), 1)
    left = lane < HD

    def stack(rows):
        zero = jnp.zeros_like(rows)
        return jnp.concatenate([jnp.where(left, rows, zero), jnp.where(left, zero, rows)], axis=0)

    def join(rows):
        return jnp.where(left, rows[:win], rows[win:])

    def attend(p, i):
        cols = pl.ds(p * PAIR, PAIR)
        here = pl.ds(i * win, win)
        around = pl.ds(i * win, 3 * win)
        q2 = stack(query[here, cols])
        d2 = stack(dattn[here, cols])
        k2 = keyed[around, cols]
        v2 = valued[around, cols]
        mask = bias[i]
        score = nt(q2, k2) * scale + jnp.concatenate([mask, mask], axis=0)
        top = jnp.max(score, axis=-1, keepdims=True)
        weight = jnp.exp(score - top)
        prob = weight * (1.0 / jnp.sum(weight, axis=-1, keepdims=True))
        probb = prob.astype(BF16)
        attended = nn(probb, v2).astype(BF16)
        att[here, :] = join(attended)
        delta = jnp.sum(d2.astype(F32) * attended.astype(F32), axis=-1, keepdims=True)
        dscore = (prob * (nt(d2, v2) - delta)).astype(BF16)
        dq[here, cols] = (join(nn(dscore, k2)) * scale).astype(BF16)
        part_k = tn(dscore, q2)
        part_v = tn(probb, d2)
        if i == 0:
            acc_k[around] = part_k
            acc_v[around] = part_v
        else:
            kept = pl.ds(i * win, 2 * win)
            fresh = pl.ds((i + 2) * win, win)
            acc_k[kept] += part_k[: 2 * win]
            acc_v[kept] += part_v[: 2 * win]
            acc_k[fresh] = part_k[2 * win :]
            acc_v[fresh] = part_v[2 * win :]

    sides = []

    def finish(p):
        cols = pl.ds(p * PAIR, PAIR)
        dk[:, cols] = (acc_k[...] * scale).astype(BF16)
        dv[:, cols] = acc_v[...].astype(BF16)
        for side, start, device in ((0, 0, down), (1, win + span, up)):
            side_send[p, side, 0] = dk[pl.ds(start, win), cols]
            side_send[p, side, 1] = dv[pl.ds(start, win), cols]
            sides.append(
                remote(
                    side_send.at[p, side], side_recv.at[p, side],
                    side_s.at[p, side], side_r.at[p, side], device,
                )
            )
        values = (
            nn(tok_t[:, pl.ds(win, span)], dq[:, cols]),
            nn(tok_t[...], dk[:, cols]),
            nn(tok_t[...], dv[:, cols]),
            tn(dout[...], att[...]),
        )
        for m, value in enumerate(values):
            if reduced:
                total[p, m] = value
            else:
                grads[p, m] = value

    rows_a, rows_b, rows_c = width // 2, width // 4, width // 8
    rows_d = width // (8 * nz)
    plans = []
    for p in range(pairs):
        (bit_b, dev_b), (bit_c, dev_c) = ((x, to_x), (y, to_y)) if p % 2 == 0 else ((y, to_y), (x, to_x))
        base_a = core * rows_a
        base_b = base_a + bit_b * rows_b
        base_c = base_b + bit_c * rows_c
        base_d = base_c + z * rows_d
        plans.append((
            (rows_a, base_a, (1 - core) * rows_a, to_core, recv_a),
            (rows_b, base_b, base_a + (1 - bit_b) * rows_b, dev_b, recv_b),
            (rows_c, base_c, base_b + (1 - bit_c) * rows_c, dev_c, recv_c),
            base_d,
        ))

    flying = {}

    def window(start, rows):
        return pl.ds(pl.multiple_of(start, TILE_ROWS), rows)

    def push(p, level):
        rows, _, other, device, landing = plans[p][level]
        part = window(other, rows)
        send[p, :, part, :] = total[p, :, part, :].astype(BF16)
        flying[p, level] = remote(
            send.at[p, :, part, :], landing.at[p], rs_s.at[p, level], rs_r.at[p, level], device
        )

    def take(p, level):
        rows, base, _, _, landing = plans[p][level]
        flying[p, level].wait()
        part = window(base, rows)
        total[p, :, part, :] += landing[p].astype(F32)

    def push_z(p):
        base_c = plans[p][2][1]
        part = window(base_c, rows_c)
        send[p, :, part, :] = total[p, :, part, :].astype(BF16)
        for step in range(1, nz):
            there = base_c + lax.rem(z + step, nz) * rows_d
            flying[p, 2 + step] = remote(
                send.at[p, :, window(there, rows_d), :], recv_d.at[p, step - 1],
                rs_s.at[p, 2 + step], rs_r.at[p, 2 + step], to_z(step),
            )

    def take_z(p):
        part = window(plans[p][3], rows_d)
        value = total[p, :, part, :]
        for step in range(1, nz):
            flying[p, 2 + step].wait()
            value = value + recv_d[p, step - 1].astype(F32)
        grads[p, :, part, :] = value.astype(BF16)
        for step in range(1, nz):
            flying[p, "z", step] = remote(
                grads.at[p, :, part, :], grads.at[p, :, part, :],
                ag_s.at[p, 2 + step], ag_r.at[p, 2 + step], to_z(step),
            )

    def spread(p, level):
        rows, base, _, device, _ = plans[p][level]
        part = window(base, rows)
        flying[p, "g", level] = remote(
            grads.at[p, :, part, :], grads.at[p, :, part, :],
            ag_s.at[p, level], ag_r.at[p, level], device,
        )

    def event(p, number):
        if number == 0:
            push(p, 0)
        elif number in (1, 2):
            take(p, number - 1)
            push(p, number)
        elif number == 3:
            take(p, 2)
            push_z(p)
        elif number == 4:
            take_z(p)
        elif number == 5:
            for step in range(1, nz):
                flying[p, "z", step].wait()
            spread(p, 2)
        elif number in (6, 7):
            flying[p, "g", 8 - number].wait()
            spread(p, 7 - number)
        elif number == 8:
            flying[p, "g", 0].wait()

    def tick(slot):
        if reduced:
            for p in range(pairs):
                number = slot - blocks * (p + 1)
                if 0 <= number <= 8:
                    event(p, number)

    slot = 0
    for p in range(pairs):
        for i in range(blocks):
            tick(slot)
            attend(p, i)
            slot += 1
        finish(p)
    for i in range(blocks):
        tick(slot)
        here = pl.ds(i * win, win)
        there = pl.ds((i + 1) * win, win)
        value = nt(dq[here], w_q[...]) + nt(dk[there], w_k[...]) + nt(dv[there], w_v[...])
        if i == 0:
            for copy in sides:
                copy.wait()
        if i in (0, blocks - 1):
            for side in ((1,) if i == 0 else (0,)):
                part_k = jnp.concatenate([side_recv[p, side, 0] for p in range(pairs)], axis=1)
                part_v = jnp.concatenate([side_recv[p, side, 1] for p in range(pairs)], axis=1)
                value = value + nt(part_k, w_k[...]) + nt(part_v, w_v[...])
        out[here] = value.astype(BF16)
        slot += 1
    while slot <= blocks * pairs + 8:
        tick(slot)
        slot += 1


def on_device(tokens, segment_ids, w_query, w_key, w_value, w_out, grad_out):
    span, width = tokens.shape[1:]
    n_ctx, n_dp = lax.axis_size("ctx"), lax.axis_size("dp")
    pairs = width // PAIR
    nz = n_ctx // 2
    reduced = n_dp == 4 and n_ctx % 2 == 0 and width // (8 * nz) >= TILE_ROWS
    ext = span + 2 * WINDOW
    vmem = pltpu.VMEM
    dma = pltpu.SemaphoreType.DMA
    few = nz if reduced else 2

    def red(*shape):
        return vmem(shape if reduced else (TILE_ROWS, 128), BF16)

    scratch = [
        vmem((2, WINDOW, width), BF16),
        vmem((2, 8, span), jnp.int32),
        vmem((8, span), jnp.int32),
        vmem((width, ext), BF16),
        vmem((span, width), BF16),
        vmem((span, width), BF16),
        vmem((ext, width), BF16),
        vmem((ext, width), BF16),
        vmem((span // WINDOW, WINDOW, 3 * WINDOW), F32),
        vmem((span, width), BF16),
        vmem((ext, width), BF16),
        vmem((ext, width), BF16),
        vmem((ext, PAIR), F32),
        vmem((ext, PAIR), F32),
        vmem((span, PAIR), BF16),
        vmem((pairs, 2, 2, WINDOW, PAIR), BF16),
        vmem((pairs, 2, 2, WINDOW, PAIR), BF16),
        vmem((pairs, 4, width, PAIR) if reduced else (8, 128), F32),
        red(pairs, 4, width, PAIR),
        red(pairs, 4, width // 2, PAIR),
        red(pairs, 4, width // 4, PAIR),
        red(pairs, 4, width // 8, PAIR),
        red(pairs, few - 1, 4, width // (8 * few), PAIR),
        dma((2,)), dma((2,)), dma((2,)), dma((2,)),
        dma((pairs, 2)), dma((pairs, 2)),
        dma((pairs, 2 + few)), dma((pairs, 2 + few)),
        dma((pairs, 2 + few)), dma((pairs, 2 + few)),
    ]
    total, grads = pl.pallas_call(
        functools.partial(kernel, n_ctx, n_dp, reduced),
        out_shape=(
            jax.ShapeDtypeStruct((span, width), BF16),
            jax.ShapeDtypeStruct((pairs, 4, width, PAIR), BF16 if reduced else F32),
        ),
        in_specs=[pl.BlockSpec(memory_space=pltpu.VMEM)] * 7,
        out_specs=(pl.BlockSpec(memory_space=pltpu.VMEM),) * 2,
        scratch_shapes=scratch,
        compiler_params=pltpu.CompilerParams(
            collective_id=0, has_side_effects=True, vmem_limit_bytes=48 * 1024 * 1024
        ),
    )(tokens[0], segment_ids, w_query, w_key, w_value, w_out, grad_out[0])
    if not reduced:
        grads = lax.psum(grads, ("ctx", "dp")).astype(BF16)
    merged = jnp.transpose(grads[:, :3], (1, 2, 0, 3)).reshape(3, width, width)
    grad_o = jnp.transpose(grads[:, 3], (0, 2, 1)).reshape(width, width)
    return (total[None], merged[0], merged[1], merged[2], grad_o)


def solution(mesh):
    return jax.shard_map(
        on_device,
        mesh=mesh,
        in_specs=(P("dp", "ctx", None), P("dp", "ctx"), P(), P(), P(), P(), P("dp", "ctx", None)),
        out_specs=(P("dp", "ctx", None), P(), P(), P(), P()),
        check_vma=False,
    )
```

time: 234 us -> 111 us (0.47)
  Pallas kernels: 0 us -> 95.2 us
  blocking collectives: 94 us -> 0 us
  matrix products: 77.8 us -> 0 us
  starting transfers between devices: 18.9 us -> 0 us
  other arithmetic: 18 us -> 0 us
  waiting for transfers between devices: 8.38 us -> 0 us
    pallas_call x0 -> x1, Pallas kernels: none -> 95.2 us  [on_device(): pl.pallas_call(functools.partial(kernel, n_ctx, n_dp, reduced), out_shape...]
    psum x1 -> x0, blocking collectives: 94 us -> none  [on_device(): lax.psum((grad_wq, grad_wk, grad_wv, grad_wo), ('ctx', 'dp'))]
    dot_general x67 -> x0, matrix products: 77.8 us -> none  [the longest x63 74.6 us: matmul(): return jnp.dot(left, right, preferred_element_type=jnp.float32)]
    ppermute x6 -> x0, starting transfers between devices: 18.9 us -> none  [the longest x2 9.39 us: extended(): lax.ppermute(lax.slice_in_dim(block, block.shape[dim] - width, None, axis...]
    reduce_sum x16 -> x0, other arithmetic: 8.77 us -> none  [the longest x8 8.47 us: head_step(): prob = weight / jnp.sum(weight, axis=-1, keepdims=True)]
    ppermute x6 -> x0, waiting for transfers between devices: 8.38 us -> none  [the longest x2 6.26 us: shifted(): return lax.ppermute(block, axis, route)]
    div x8 -> x0, other arithmetic: 7.25 us -> none  [head_step(): prob = weight / jnp.sum(weight, axis=-1, keepdims=True)]
    reshape x3 -> x0, local copies, waits for them, and re-layouts: 4.67 us -> none  [split_heads(): return jnp.transpose(values.reshape(length, H, HD), (1, 0, 2))]
  transfers between devices with their start and end apart: 6 -> 0, of which waited for: 3 -> 0; matrix products, arithmetic and copies ran while one was open for 2% -> 0% of each run, Pallas kernels for 0% -> 0%
where the time goes in v1:
time: 111 us; the launch traced here: 110 us
  Pallas kernels  95.2 us (86%)
  local copies, waits for them, and re-layouts  14.4 us (13%)
    pallas_call x1, Pallas kernels, on_device(): pl.pallas_call(functools.partial(kernel, n_ctx, n_dp, reduced), out_shape...  95.2 us
    unnamed x18, local copies, waits for them, and re-layouts  10.7 us
    slice x4, local copies, waits for them, and re-layouts, on_device(): return (total[None], merged[0], merged[1], merged[2], grad_o)  2.57 us

profile of v1, /device:TPU:0, one launch (start us, length us, event | category | flops | bytes accessed | tf_op | source)
XLA Modules:
  0.0 110.3 jit_solution(1134300082864725228)
XLA Ops:
  0.6 0.0 copy-start
  0.6 1.0 copy-done
  1.7 0.0 copy-start.1
  1.7 1.0 copy-done.1
  2.7 0.0 copy-start.2
  2.7 1.0 copy-done.2
  3.8 0.0 copy-start.3
  3.8 1.0 copy-done.3
  4.8 0.0 copy-start.4
  4.8 1.0 copy-done.4
  5.8 0.0 copy-start.5
  5.8 1.0 copy-done.5
  6.9 0.0 copy-start.6
  6.9 0.7 copy-done.6
  7.6 95.2 %shard_map.110 = (bf16[512,512]{1,0:T(8,128)(2,1)S(1)}, bf16[4,4,512,128]{3,2,1,0:T(8,128)(2,1)S(1)}) custom-call(bf16[512,512]{1,0:T(8,128)(2,1)S(1)} %bitcast.14, s32[1,512]{1,0:T(1,128)S(1)} %copy-done.6, bf16[512,512]{1,0:T(8,128)(2,1)S(1)} %copy-done.1, bf16[512,512]{1,0:T(8,128)(2,1)S(1)} %copy-done.2, bf16[512,512]{1,0:T(8,128)(2,1)S(1)} %copy-done.3, ...), custom_call_target="tpu_custom_call" | custom-call | tf_op jit(solution)/shard_map/pallas_call | solution.py:352
  102.8 0.1 slice_bitcast_fusion
  102.9 1.0 copy.15
  103.9 0.9 fusion
  104.8 1.2 %copy.14 = bf16[1,512,4,128]{1,3,2,0:T(8,128)(2,1)S(1)} copy(bf16[1,512,4,128]{3,1,0,2:T(8,128)(2,1)} %get-tuple-element.14) | data formatting | bytes 1048576 | tf_op jit(solution)/shard_map/slice | solution.py:369
  106.1 1.0 copy.18
  107.1 0.2 copy.13
  107.3 1.0 copy.17
  108.3 0.2 copy.12
  108.5 1.0 copy.16
  109.5 0.8 copy.20
  (1 shorter events, 0.0 us)
Async XLA Ops:
  0.6 1.0 copy-start
  1.7 1.0 copy-start.1
  2.7 1.0 copy-start.2
  3.8 1.0 copy-start.3
  4.8 1.0 copy-start.4
  5.8 1.0 copy-start.5
  6.9 0.7 copy-start.6

commit v2 on v1

--- a/solution.py
+++ b/solution.py
@@ -34,8 +34,9 @@
 
 def kernel(
     n_ctx, n_dp, reduced,
-    tok, seg_row, w_q, w_k, w_v, w_o, dout,
+    tok_hbm, seg_hbm, wq_hbm, wk_hbm, wv_hbm, wo_hbm, dout_hbm,
     out, grads,
+    tok, seg_row, w_q, w_k, w_v, w_o, dout, load,
     halo, seg_halo, seg_own, tok_t, query, dattn, keyed, valued, bias,
     dq, dk, dv, acc_k, acc_v, att,
     side_send, side_recv,
@@ -44,6 +45,13 @@
 ):
     span, width = tok.shape
     win = WINDOW
+    loads = {}
+    for n, (name, src, dst) in enumerate((
+        ("seg", seg_hbm, seg_row), ("tok", tok_hbm, tok), ("q", wq_hbm, w_q), ("k", wk_hbm, w_k),
+        ("v", wv_hbm, w_v), ("o", wo_hbm, w_o), ("dout", dout_hbm, dout),
+    )):
+        loads[name] = pltpu.make_async_copy(src, dst, load.at[n])
+        loads[name].start()
     blocks = span // win
     pairs = width // PAIR
     ctx = lax.axis_index("ctx")
@@ -70,6 +78,7 @@
     for partner in partners:
         pl.semaphore_signal(barrier, inc=1, device_id=partner, device_id_type=MESH)
 
+    loads["seg"].wait()
     seg_own[...] = jnp.broadcast_to(seg_row[...], seg_own.shape)
     pl.semaphore_wait(barrier, len(partners))
 
@@ -81,38 +90,23 @@
         return copy
 
     first = [
-        remote(tok.at[pl.ds(span - win, win)], halo.at[0], halo_s.at[0], halo_r.at[0], up),
-        remote(tok.at[pl.ds(0, win)], halo.at[1], halo_s.at[1], halo_r.at[1], down),
+        remote(tok_hbm.at[pl.ds(span - win, win)], halo.at[0], halo_s.at[0], halo_r.at[0], up),
+        remote(tok_hbm.at[pl.ds(0, win)], halo.at[1], halo_s.at[1], halo_r.at[1], down),
         remote(seg_own, seg_halo.at[0], seg_s.at[0], seg_r.at[0], up),
         remote(seg_own, seg_halo.at[1], seg_s.at[1], seg_r.at[1], down),
     ]
 
+    loads["tok"].wait()
+    tok_t[:, pl.ds(win, span)] = tok[...].T
+    loads["q"].wait()
     query[...] = nn(tok[...], w_q[...]).astype(BF16)
+    loads["k"].wait()
     keyed[pl.ds(win, span)] = nn(tok[...], w_k[...]).astype(BF16)
+    loads["v"].wait()
     valued[pl.ds(win, span)] = nn(tok[...], w_v[...]).astype(BF16)
+    loads["o"].wait()
+    loads["dout"].wait()
     dattn[...] = nt(dout[...], w_o[...]).astype(BF16)
-    tok_t[:, pl.ds(win, span)] = tok[...].T
-
-    for copy in first:
-        copy.wait()
-    for side, start in ((0, 0), (1, win + span)):
-        rows = halo[side]
-        keyed[pl.ds(start, win)] = nn(rows, w_k[...]).astype(BF16)
-        valued[pl.ds(start, win)] = nn(rows, w_v[...]).astype(BF16)
-        tok_t[:, pl.ds(start, win)] = rows.T
-
-    own = seg_row[...].astype(F32)
-    low = jnp.where(ctx > 0, seg_halo[0, 0:1, span - win :].astype(F32), -1.0)
-    high = jnp.where(ctx < n_ctx - 1, seg_halo[1, 0:1, :win].astype(F32), -1.0)
-    seg_all = jnp.concatenate([low, own, high], axis=1)
-    q_pos = lax.broadcasted_iota(jnp.int32, (win, 3 * win), 0)
-    k_pos = lax.broadcasted_iota(jnp.int32, (win, 3 * win), 1)
-    near = (k_pos >= q_pos) & (k_pos <= q_pos + 2 * win)
-    for i in range(blocks):
-        column = jnp.broadcast_to(own[:, i * win : (i + 1) * win], (win, win)).T
-        column = jnp.concatenate([column] * 3, axis=1)
-        same = column == seg_all[:, i * win : (i + 3) * win]
-        bias[i] = jnp.where(near & same, 0.0, -1e30)
 
     scale = float(HD) ** (-0.5)
     lane = lax.broadcasted_iota(jnp.int32, (win, PAIR), 1)
@@ -140,29 +134,50 @@
         prob = weight * (1.0 / jnp.sum(weight, axis=-1, keepdims=True))
         probb = prob.astype(BF16)
         attended = nn(probb, v2).astype(BF16)
-        att[here, :] = join(attended)
+        att[p, here, :] = join(attended)
         delta = jnp.sum(d2.astype(F32) * attended.astype(F32), axis=-1, keepdims=True)
         dscore = (prob * (nt(d2, v2) - delta)).astype(BF16)
         dq[here, cols] = (join(nn(dscore, k2)) * scale).astype(BF16)
         part_k = tn(dscore, q2)
         part_v = tn(probb, d2)
-        if i == 0:
-            acc_k[around] = part_k
-            acc_v[around] = part_v
-        else:
-            kept = pl.ds(i * win, 2 * win)
-            fresh = pl.ds((i + 2) * win, win)
-            acc_k[kept] += part_k[: 2 * win]
-            acc_v[kept] += part_v[: 2 * win]
-            acc_k[fresh] = part_k[2 * win :]
-            acc_v[fresh] = part_v[2 * win :]
+        acc_k[p, around] += part_k
+        acc_v[p, around] += part_v
+
+    own = seg_row[...].astype(F32)
+    q_pos = lax.broadcasted_iota(jnp.int32, (win, 3 * win), 0)
+    k_pos = lax.broadcasted_iota(jnp.int32, (win, 3 * win), 1)
+    near = (k_pos >= q_pos) & (k_pos <= q_pos + 2 * win)
+
+    def masked(i, keys):
+        column = jnp.broadcast_to(own[:, i * win : (i + 1) * win], (win, win)).T
+        column = jnp.concatenate([column] * 3, axis=1)
+        bias[i] = jnp.where(near & (column == keys), 0.0, -1e30)
+
+    acc_k[...] = jnp.zeros_like(acc_k)
+    acc_v[...] = jnp.zeros_like(acc_v)
+    for i in range(1, blocks - 1):
+        masked(i, own[:, (i - 1) * win : (i + 2) * win])
+        for p in range(pairs):
+            attend(p, i)
+
+    for copy in first:
+        copy.wait()
+    for side, start in ((0, 0), (1, win + span)):
+        rows = halo[side]
+        keyed[pl.ds(start, win)] = nn(rows, w_k[...]).astype(BF16)
+        valued[pl.ds(start, win)] = nn(rows, w_v[...]).astype(BF16)
+        tok_t[:, pl.ds(start, win)] = rows.T
+    low = jnp.where(ctx > 0, seg_halo[0, 0:1, span - win :].astype(F32), -1.0)
+    high = jnp.where(ctx < n_ctx - 1, seg_halo[1, 0:1, :win].astype(F32), -1.0)
+    masked(0, jnp.concatenate([low, own[:, : 2 * win]], axis=1))
+    masked(blocks - 1, jnp.concatenate([own[:, span - 2 * win :], high], axis=1))
 
     sides = []
 
     def finish(p):
         cols = pl.ds(p * PAIR, PAIR)
-        dk[:, cols] = (acc_k[...] * scale).astype(BF16)
-        dv[:, cols] = acc_v[...].astype(BF16)
+        dk[:, cols] = (acc_k[p] * scale).astype(BF16)
+        dv[:, cols] = acc_v[p].astype(BF16)
         for side, start, device in ((0, 0, down), (1, win + span, up)):
             side_send[p, side, 0] = dk[pl.ds(start, win), cols]
             side_send[p, side, 1] = dv[pl.ds(start, win), cols]
@@ -176,19 +191,20 @@
             nn(tok_t[:, pl.ds(win, span)], dq[:, cols]),
             nn(tok_t[...], dk[:, cols]),
             nn(tok_t[...], dv[:, cols]),
-            tn(dout[...], att[...]),
         )
+        place = total if reduced else grads
         for m, value in enumerate(values):
-            if reduced:
-                total[p, m] = value
-            else:
-                grads[p, m] = value
+            place[p, m] = value
+        value = tn(att[p], dout[...])
+        for j in range(width // PAIR):
+            block = pl.ds(j * PAIR, PAIR)
+            place[p, 3, block] = value[:, j * PAIR : (j + 1) * PAIR]
 
     rows_a, rows_b, rows_c = width // 2, width // 4, width // 8
     rows_d = width // (8 * nz)
     plans = []
     for p in range(pairs):
-        (bit_b, dev_b), (bit_c, dev_c) = ((x, to_x), (y, to_y)) if p % 2 == 0 else ((y, to_y), (x, to_x))
+        (bit_b, dev_b), (bit_c, dev_c) = ((y, to_y), (x, to_x))
         base_a = core * rows_a
         base_b = base_a + bit_b * rows_b
         base_c = base_b + bit_c * rows_c
@@ -272,38 +288,62 @@
         elif number == 8:
             flying[p, "g", 0].wait()
 
+    starts = (12, 17, 21, 25, 29, 35, 38)
+    due = sorted(
+        (slot, p, number)
+        for p in range(pairs)
+        for number, slot in enumerate((4 + 4 * p, 7 + 4 * p) + tuple(s + 5 * p for s in starts))
+    )
+
     def tick(slot):
-        if reduced:
-            for p in range(pairs):
-                number = slot - blocks * (p + 1)
-                if 0 <= number <= 8:
-                    event(p, number)
-
-    slot = 0
-    for p in range(pairs):
-        for i in range(blocks):
-            tick(slot)
-            attend(p, i)
-            slot += 1
-        finish(p)
-    for i in range(blocks):
-        tick(slot)
+        while reduced and due and due[0][0] <= slot:
+            _, p, number = due.pop(0)
+            event(p, number)
+
+    def input_block(i):
         here = pl.ds(i * win, win)
         there = pl.ds((i + 1) * win, win)
         value = nt(dq[here], w_q[...]) + nt(dk[there], w_k[...]) + nt(dv[there], w_v[...])
-        if i == 0:
-            for copy in sides:
-                copy.wait()
         if i in (0, blocks - 1):
-            for side in ((1,) if i == 0 else (0,)):
+            for side in (1,) if i == 0 else (0,):
                 part_k = jnp.concatenate([side_recv[p, side, 0] for p in range(pairs)], axis=1)
                 part_v = jnp.concatenate([side_recv[p, side, 1] for p in range(pairs)], axis=1)
                 value = value + nt(part_k, w_k[...]) + nt(part_v, w_v[...])
         out[here] = value.astype(BF16)
+
+    slot = 0
+    for p in range(pairs):
+        for i in (0, blocks - 1):
+            tick(slot)
+            attend(p, i)
+            slot += 2
+        finish(p)
+    for i in range(1, blocks - 1):
+        tick(slot)
+        input_block(i)
         slot += 1
-    while slot <= blocks * pairs + 8:
-        tick(slot)
-        slot += 1
+    tick(blocks * pairs + 10)
+    for copy in sides:
+        copy.wait()
+    input_block(0)
+    input_block(blocks - 1)
+    tick(1000)
+
+
+def lay_out(total, grads, out, g_q, g_k, g_v, g_o, sem):
+    pairs, _, width, _ = grads.shape
+    copies = [(total, out)]
+    for p in range(pairs):
+        cols = pl.ds(p * PAIR, PAIR)
+        copies += [(grads.at[p, m], g.at[:, cols]) for m, g in enumerate((g_q, g_k, g_v))]
+        for j in range(width // PAIR):
+            block = pl.ds(j * PAIR, PAIR)
+            copies.append((grads.at[p, 3, block], g_o.at[cols, block]))
+    flying = [pltpu.make_async_copy(src, dst, sem.at[n]) for n, (src, dst) in enumerate(copies)]
+    for copy in flying:
+        copy.start()
+    for copy in flying:
+        copy.wait()
 
 
 def on_device(tokens, segment_ids, w_query, w_key, w_value, w_out, grad_out):
@@ -320,7 +360,13 @@
     def red(*shape):
         return vmem(shape if reduced else (TILE_ROWS, 128), BF16)
 
+    weights = vmem((width, width), BF16)
     scratch = [
+        vmem((span, width), BF16),
+        vmem((1, span), jnp.int32),
+        weights, weights, weights, weights,
+        vmem((span, width), BF16),
+        dma((7,)),
         vmem((2, WINDOW, width), BF16),
         vmem((2, 8, span), jnp.int32),
         vmem((8, span), jnp.int32),
@@ -333,9 +379,9 @@
         vmem((span, width), BF16),
         vmem((ext, width), BF16),
         vmem((ext, width), BF16),
-        vmem((ext, PAIR), F32),
-        vmem((ext, PAIR), F32),
-        vmem((span, PAIR), BF16),
+        vmem((pairs, ext, PAIR), F32),
+        vmem((pairs, ext, PAIR), F32),
+        vmem((pairs, span, PAIR), BF16),
         vmem((pairs, 2, 2, WINDOW, PAIR), BF16),
         vmem((pairs, 2, 2, WINDOW, PAIR), BF16),
         vmem((pairs, 4, width, PAIR) if reduced else (8, 128), F32),
@@ -355,18 +401,24 @@
             jax.ShapeDtypeStruct((span, width), BF16),
             jax.ShapeDtypeStruct((pairs, 4, width, PAIR), BF16 if reduced else F32),
         ),
-        in_specs=[pl.BlockSpec(memory_space=pltpu.VMEM)] * 7,
+        in_specs=[pl.BlockSpec(memory_space=pl.ANY)] * 7,
         out_specs=(pl.BlockSpec(memory_space=pltpu.VMEM),) * 2,
         scratch_shapes=scratch,
         compiler_params=pltpu.CompilerParams(
-            collective_id=0, has_side_effects=True, vmem_limit_bytes=48 * 1024 * 1024
+            collective_id=0, has_side_effects=True, vmem_limit_bytes=60 * 1024 * 1024
         ),
     )(tokens[0], segment_ids, w_query, w_key, w_value, w_out, grad_out[0])
     if not reduced:
         grads = lax.psum(grads, ("ctx", "dp")).astype(BF16)
-    merged = jnp.transpose(grads[:, :3], (1, 2, 0, 3)).reshape(3, width, width)
-    grad_o = jnp.transpose(grads[:, 3], (0, 2, 1)).reshape(width, width)
-    return (total[None], merged[0], merged[1], merged[2], grad_o)
+    square = jax.ShapeDtypeStruct((width, width), BF16)
+    total, *grads = pl.pallas_call(
+        lay_out,
+        out_shape=(jax.ShapeDtypeStruct((span, width), BF16),) + (square,) * 4,
+        in_specs=[pl.BlockSpec(memory_space=pltpu.VMEM)] * 2,
+        out_specs=(pl.BlockSpec(memory_space=pl.ANY),) * 5,
+        scratch_shapes=[dma((1 + pairs * (3 + width // PAIR),))],
+    )(total, grads)
+    return (total[None], *grads)
 
 
 def solution(mesh):

time: 111 us -> 66.9 us (0.60)
  Pallas kernels: 95.2 us -> 65.9 us
  local copies, waits for them, and re-layouts: 14.4 us -> 0 us
    pallas_call x1, Pallas kernels: 95.2 us -> 62.4 us  [on_device(): pl.pallas_call(functools.partial(kernel, n_ctx, n_dp, reduced), out_shape...]
    unnamed x18 -> x0, local copies, waits for them, and re-layouts: 10.7 us -> none
    pallas_call x0 -> x1, Pallas kernels: none -> 3.48 us  [on_device(): pl.pallas_call(lay_out, out_shape=(jax.ShapeDtypeStruct((span, width), BF...]
    slice x4 -> x0, local copies, waits for them, and re-layouts: 2.57 us -> none  [on_device(): return (total[None], merged[0], merged[1], merged[2], grad_o)]
    transpose x3 -> x0, local copies, waits for them, and re-layouts: 1.15 us -> none  [the longest x2 1.04 us: on_device(): grad_o = jnp.transpose(grads[:, 3], (0, 2, 1)).reshape(width, width)]
where the time goes in v2:
time: 66.9 us; the launch traced here: 66.7 us
  Pallas kernels  65.9 us (99%)
  between operations  0.8 us (1%)
    pallas_call x1, Pallas kernels, on_device(): pl.pallas_call(functools.partial(kernel, n_ctx, n_dp, reduced), out_shape...  62.4 us
    pallas_call x1, Pallas kernels, on_device(): pl.pallas_call(lay_out, out_shape=(jax.ShapeDtypeStruct((span, width), BF...  3.48 us

profile of v2, /device:TPU:0, one launch (start us, length us, event | category | flops | bytes accessed | tf_op | source)
XLA Modules:
  0.0 66.7 jit_solution(3306040096666062259)
XLA Ops:
  0.6 62.4 %shard_map.110 = (bf16[512,512]{1,0:T(8,128)(2,1)}, bf16[4,4,512,128]{3,2,1,0:T(8,128)(2,1)}) custom-call(bf16[512,512]{1,0:T(8,128)(2,1)} %bitcast.3, s32[1,512]{1,0:T(1,128)} %seg_hbm.1, bf16[512,512]{1,0:T(8,128)(2,1)} %wq_hbm.1, bf16[512,512]{1,0:T(8,128)(2,1)} %wk_hbm.1, bf16[512,512]{1,0:T(8,128)(2,1)} %wv_hbm.1, bf16[512,512]{1,0:T(8,128)(2,1)} %wo_hbm.1, ...), custom_call_target="tpu_custom_call" | custom-call | tf_op jit(solution)/shard_map/pallas_call | solution.py:398
  63.0 3.5 %shard_map.111 = (bf16[512,512]{1,0:T(8,128)(2,1)}, bf16[512,512]{1,0:T(8,128)(2,1)}, bf16[512,512]{1,0:T(8,128)(2,1)}, bf16[512,512]{1,0:T(8,128)(2,1)}, bf16[512,512]{1,0:T(8,128)(2,1)}) custom-call(bf16[512,512]{1,0:T(8,128)(2,1)} %get-tuple-element.12.total, bf16[4,4,512,128]{3,2,1,0:T(8,128)(2,1)} %get-tuple-element.13.grads), custom_call_target="tpu_custom_call" | custom-call | tf_op jit(solution)/shard_map/pallas_call | solution.py:414

commit v3 on v2

--- a/solution.py
+++ b/solution.py
@@ -414,8 +414,9 @@
     total, *grads = pl.pallas_call(
         lay_out,
         out_shape=(jax.ShapeDtypeStruct((span, width), BF16),) + (square,) * 4,
-        in_specs=[pl.BlockSpec(memory_space=pltpu.VMEM)] * 2,
+        in_specs=[pl.BlockSpec(memory_space=pl.ANY)] * 2,
         out_specs=(pl.BlockSpec(memory_space=pl.ANY),) * 5,
+        compiler_params=pltpu.CompilerParams(vmem_limit_bytes=60 * 1024 * 1024),
         scratch_shapes=[dma((1 + pairs * (3 + width // PAIR),))],
     )(total, grads)
     return (total[None], *grads)

time: 66.9 us -> 144 us (2.15)
  Pallas kernels: 65.9 us -> 143 us
    pallas_call x1, Pallas kernels: 3.48 us -> 80.8 us  [on_device(): pl.pallas_call(lay_out, out_shape=(jax.ShapeDtypeStruct((span, width), BF...]
where the time goes in v3:
time: 144 us
  Pallas kernels  143 us (99%)
    pallas_call x1, Pallas kernels, on_device(): pl.pallas_call(lay_out, out_shape=(jax.ShapeDtypeStruct((span, width), BF...  80.8 us
    pallas_call x1, Pallas kernels, on_device(): pl.pallas_call(functools.partial(kernel, n_ctx, n_dp, reduced), out_shape...  62.4 us

profile of v3, /device:TPU:0, one launch (start us, length us, event | category | flops | bytes accessed | tf_op | source)
XLA Modules:
  0.0 144.0 jit_solution(15170487908232170911)
XLA Ops:
  0.6 62.4 %shard_map.110 = (bf16[512,512]{1,0:T(8,128)(2,1)}, bf16[4,4,512,128]{3,2,1,0:T(8,128)(2,1)}) custom-call(bf16[512,512]{1,0:T(8,128)(2,1)} %bitcast.3, s32[1,512]{1,0:T(1,128)} %seg_hbm.1, bf16[512,512]{1,0:T(8,128)(2,1)} %wq_hbm.1, bf16[512,512]{1,0:T(8,128)(2,1)} %wk_hbm.1, bf16[512,512]{1,0:T(8,128)(2,1)} %wv_hbm.1, bf16[512,512]{1,0:T(8,128)(2,1)} %wo_hbm.1, ...), custom_call_target="tpu_custom_call" | custom-call | tf_op jit(solution)/shard_map/pallas_call | solution.py:398
  63.0 80.8 %shard_map.111 = (bf16[512,512]{1,0:T(8,128)(2,1)}, bf16[512,512]{1,0:T(8,128)(2,1)}, bf16[512,512]{1,0:T(8,128)(2,1)}, bf16[512,512]{1,0:T(8,128)(2,1)}, bf16[512,512]{1,0:T(8,128)(2,1)}) custom-call(bf16[512,512]{1,0:T(8,128)(2,1)} %get-tuple-element.12.total, bf16[4,4,512,128]{3,2,1,0:T(8,128)(2,1)} %get-tuple-element.13.grads), custom_call_target="tpu_custom_call" | custom-call | tf_op jit(solution)/shard_map/pallas_call | solution.py:414
